TPU v7x, 512 devices: a whole 4x4x16 slice. The times are simulated.
512 devices in a mesh: expert: 16 (over x_hi, y, core), tensor: 32 (over x_lo, z).
Axes of the slice: x: 4 (x_hi: 2, x_lo: 2; x = x_hi * 2 + x_lo), y: 4, z: 16, core: 2. Of those that a mesh axis runs over, the one named last changes fastest.
Arguments:
- token_grads: bfloat16 [2048, 5120], P('expert', 'tensor'), may hold values from -4 to 4
- combine: float32 [2048, 6], P('expert'), may hold values from 0.1 to 1
- routes: int32 [2048, 6], P('expert'), may hold values from 0 to 15, all different within a row; in each aligned block of 128 rows (0 to 127, 128 to 255, ...) at most 96 rows name the same one
- bin_inputs: bfloat16 [16, 1024, 5120], P('expert', None, 'tensor'), may hold values from -6 to 6
- gate_pre: bfloat16 [16, 1536, 1024], P('expert', 'tensor'), may hold values from -6 to 6
- up_pre: bfloat16 [16, 1536, 1024], P('expert', 'tensor'), may hold values from -6 to 6
- gate_weight: bfloat16 [16, 5120, 1536], P('expert', 'tensor'), may hold values from -0.15625 to 0.15625
- up_weight: bfloat16 [16, 5120, 1536], P('expert', 'tensor'), may hold values from -0.15625 to 0.15625
- down_weight: bfloat16 [16, 5120, 1536], P('expert', 'tensor'), may hold values from -0.078125 to 0.078125
Outputs:
- token_grad: bfloat16 [2048, 5120], P('expert', 'tensor')
- gate_grad: bfloat16 [16, 5120, 1536], P('expert', 'tensor')
- up_grad: bfloat16 [16, 5120, 1536], P('expert', 'tensor')
- down_grad: bfloat16 [16, 5120, 1536], P('expert', 'tensor')
Inputs may be any that keep to these rules, and one draw needn't show every extreme that they name: `routes`: each token names 6 different experts. Within the 128 tokens of one index of the expert axis no expert is named by more than 96 tokens.
All inputs are finite; a program needn't handle non-finite values.
Results may differ from a plain program's by a relative error of at most 0.0064.
Values may be sent and summed in bfloat16 or wider, within the bound.
A program may use at most 64 MiB of HBM per device.

v0:
```python
import jax
import jax.numpy as jnp
from jax import lax
from jax.sharding import PartitionSpec as P

EXPERTS = 16
CAP = 64


def route_slots(block):
    flat_routes = block.reshape(-1)
    expert_ids = jnp.arange(EXPERTS, dtype=jnp.int32)
    onehot = (flat_routes[:, None] == expert_ids[None, :]).astype(jnp.int32)
    earlier = jnp.cumsum(onehot, axis=0) - onehot
    slot_rank = jnp.sum(earlier * onehot, axis=1)
    return (flat_routes, slot_rank, slot_rank < CAP)


def activate(hidden_grad, gate_pre, up_pre):
    gate_vals = gate_pre.astype(jnp.float32)
    up_vals = up_pre.astype(jnp.float32)
    sigmoid_gate = 1.0 / (1.0 + jnp.exp(-gate_vals))
    activated = gate_vals * sigmoid_gate
    hidden = (activated * up_vals).astype(jnp.bfloat16)
    up_delta = (hidden_grad * activated).astype(jnp.bfloat16)
    gate_delta = (
        hidden_grad * up_vals * sigmoid_gate * (1.0 + gate_vals * (1.0 - sigmoid_gate))
    ).astype(jnp.bfloat16)
    return (hidden, gate_delta, up_delta)


def body(
    token_grads, combine, routes, bin_inputs, gate_pre, up_pre, gate_weight, up_weight, down_weight
):
    width_shard = token_grads.shape[1]
    flat_routes, slot_rank, kept_mask = route_slots(routes)
    target = jnp.where(kept_mask, flat_routes * CAP + slot_rank, -1).reshape(routes.shape)
    slot_ids = jnp.arange(EXPERTS * CAP, dtype=jnp.int32)
    matches = slot_ids[:, None, None] == target[None, :, :]
    weighted = jnp.sum(jnp.where(matches, combine[None, :, :], jnp.float32(0.0)), axis=2)
    placed = jnp.dot(weighted, token_grads.astype(jnp.float32), precision=lax.Precision.HIGHEST)
    placed = placed.astype(jnp.bfloat16).reshape(EXPERTS, CAP, width_shard)
    binned = lax.all_to_all(placed, "expert", split_axis=0, concat_axis=1, tiled=True)
    hidden_grad = jnp.einsum(
        "ebd,edf->efb", binned, down_weight, preferred_element_type=jnp.float32
    )
    hidden_total = lax.psum(hidden_grad, "tensor")
    gate_all, up_all = (
        lax.all_gather(gate_pre, "tensor", axis=1, tiled=True),
        lax.all_gather(up_pre, "tensor", axis=1, tiled=True),
    )
    hidden, gate_delta, up_delta = activate(hidden_total, gate_all, up_all)
    bin_back = (
        jnp.einsum("efb,edf->ebd", gate_delta, gate_weight, preferred_element_type=jnp.float32)
        + jnp.einsum("efb,edf->ebd", up_delta, up_weight, preferred_element_type=jnp.float32)
    ).astype(jnp.bfloat16)
    down_grad = jnp.einsum(
        "ebd,efb->edf", binned, hidden, preferred_element_type=jnp.float32
    ).astype(jnp.bfloat16)
    gate_grad = jnp.einsum(
        "ebd,efb->edf", bin_inputs, gate_delta, preferred_element_type=jnp.float32
    ).astype(jnp.bfloat16)
    up_grad = jnp.einsum(
        "ebd,efb->edf", bin_inputs, up_delta, preferred_element_type=jnp.float32
    ).astype(jnp.bfloat16)
    returned = lax.all_to_all(bin_back, "expert", split_axis=1, concat_axis=0, tiled=True)
    pick_mask = jnp.any(matches, axis=2).astype(jnp.bfloat16)
    token_grad = jnp.dot(
        pick_mask.T,
        returned.reshape(EXPERTS * CAP, width_shard),
        preferred_element_type=jnp.float32,
    )
    return (token_grad.astype(jnp.bfloat16), gate_grad, up_grad, down_grad)


def solution(mesh):
    return jax.shard_map(
        body,
        mesh=mesh,
        in_specs=(
            P("expert", "tensor"),
            P("expert", None),
            P("expert", None),
            P("expert", None, "tensor"),
            P("expert", "tensor", None),
            P("expert", "tensor", None),
            P("expert", "tensor", None),
            P("expert", "tensor", None),
            P("expert", "tensor", None),
        ),
        out_specs=(
            P("expert", "tensor"),
            P("expert", "tensor", None),
            P("expert", "tensor", None),
            P("expert", "tensor", None),
        ),
        check_vma=False,
    )
```

profile of v0, /device:TPU:1, one launch (start us, length us, event | category | flops | bytes accessed | tf_op | source)
XLA Modules:
  0.0 606.9 jit_solution(1727596532533135540)
XLA Ops:
  9.8 1.7 reduce-window.6
  12.9 1.1 select_reduce_fusion
  14.0 1.2 convolution_convert_fusion.1
  15.5 20.7 %all_to_all.8 = bf16[16,64,160]{2,1,0:T(8,128)(2,1)S(1)} all-to-all(bf16[16,64,160]{2,1,0:T(8,128)(2,1)S(1)} %bitcast.92), channel_id=1, replica_groups=mesh['expert'=16,'tensor'=32] {'expert'}, dimensions={0} | all-to-all | bytes 655360 | tf_op jit(solution)/shard_map/all_to_all | solution.py:43
  36.2 3.6 convolution_bitcast_fusion
  40.3 91.9 %all-gather.3.cloned.1.call-done = bf16[1,1536,1024]{2,1,0:T(8,128)(2,1)} async-done(((bf16[1,48,1024]{2,1,0:T(8,128)(2,1)}), bf16[1,1536,1024]{2,1,0:T(8,128)(2,1)}) %all-gather.3.cloned.1.call-update) | async-done | bytes 3145744 | tf_op jit(solution)/shard_map/all_gather | solution.py:50
  132.2 4.7 copy.56
  137.0 125.0 %all-gather.5.cloned.1.call-done = bf16[1,1536,1024]{2,1,0:T(8,128)(2,1)} async-done(((bf16[1,48,1024]{2,1,0:T(8,128)(2,1)}), bf16[1,1536,1024]{2,1,0:T(8,128)(2,1)}) %all-gather.5.cloned.1.call-update) | async-done | bytes 3145744 | tf_op jit(solution)/shard_map/all_gather | solution.py:49
  261.9 4.7 copy.57
  266.6 5.9 fusion.23
  272.5 272.5 %all-reduce.2.cloned.1.call-done = f32[1,1536,1024]{1,2,0:T(8,128)} async-done(((f32[1,1536,1024]{1,2,0:T(8,128)}), f32[1,1536,1024]{1,2,0:T(8,128)}) %all-reduce.2.cloned.1.call-update) | async-done | bytes 6291472 | tf_op jit(solution)/shard_map/psum | solution.py:47
  545.1 6.2 %fusion.2 = (bf16[1,1536,1024]{1,2,0:T(8,128)(2,1)S(1)}, bf16[1536,1024]{0,1:T(8,128)(2,1)S(1)}) fusion(f32[1,1536,1024]{1,2,0:T(8,128)} %all-reduce.2.cloned.1.call-done, bf16[1,1536,1024]{1,2,0:T(8,128)(2,1)} %copy.56, bf16[1,1536,1024]{1,2,0:T(8,128)(2,1)} %copy.57), kind=kLoop, calls=%fused_computation.7 | loop fusion | flops 23592960 | bytes 18874368 | tf_op jit(solution)/shard_map/convert_element_type | solution.py:28
  551.3 1.7 copy-done.3
  553.0 1.2 fusion.39
  554.2 1.2 fusion.36
  555.3 0.8 copy.58
  556.7 4.0 reduce.2
  560.7 1.5 reshape.102
  562.3 26.5 %all-to-all-start.1 = ((bf16[16,2,5120]{2,1,0:T(2,128)(2,1)}), bf16[16,2,5120]{2,1,0:T(2,128)(2,1)S(1)}, u32[]{:S(2)}, u32[]{:S(2)}) async-start(bf16[16,2,5120]{2,1,0:T(2,128)(2,1)} %reshape.102), calls=%async_computation.1 | async-start | bytes 655360 | tf_op jit(solution)/shard_map/all_to_all | solution.py:66
  588.8 3.5 fusion.26
  592.3 1.5 fusion.27
  593.8 4.2 all-to-all-done.1
  598.0 0.9 reshape.103
  599.5 0.9 convolution_convert_fusion.2
  (35 shorter events, 5.8 us)
Async XLA Ops:
  7.2 29.0 %copy-start = (bf16[1,160,1536]{2,1,0:T(8,128)(2,1)S(1)}, bf16[1,160,1536]{2,1,0:T(8,128)(2,1)}, u32[]{:S(2)}) copy-start(bf16[1,160,1536]{2,1,0:T(8,128)(2,1)} %param.17) | copy-start | bytes 1474564
  7.2 125.1 %all-gather.3.cloned.1.call-start = ((), (), s32[]{:S(2)}) async-start(), calls=%async_computation.3 | async-start | bytes 3244032 | tf_op jit(solution)/shard_map/all_gather | solution.py:50
  7.9 254.0 %all-gather.5.cloned.1.call-start = ((), (), s32[]{:S(2)}) async-start(), calls=%async_computation.4 | async-start | bytes 3244032 | tf_op jit(solution)/shard_map/all_gather | solution.py:49
  8.7 536.4 %all-reduce.2.cloned.1.call-start = ((), (), s32[]{:S(2)}) async-start(), calls=%async_computation.2 | async-start | bytes 12582912 | tf_op jit(solution)/shard_map/psum | solution.py:47
  272.5 280.4 %copy-start.5 = (bf16[1,160,1536]{2,1,0:T(8,128)(2,1)S(1)}, bf16[1,160,1536]{2,1,0:T(8,128)(2,1)}, u32[]{:S(2)}) copy-start(bf16[1,160,1536]{2,1,0:T(8,128)(2,1)} %param.16) | copy-start | bytes 1474564
  551.3 1.7 copy-start.3
  551.3 2.9 copy-start.1
  551.3 2.9 copy-start.6
  555.3 33.5 %copy-start.4 = (bf16[1,1024,160]{1,2,0:T(8,128)(2,1)S(1)}, bf16[1,1024,160]{1,2,0:T(8,128)(2,1)}, u32[]{:S(2)}) copy-start(bf16[1,1024,160]{1,2,0:T(8,128)(2,1)} %param.12) | copy-start | bytes 983044
  562.3 35.7 %all-to-all-start.1 = ((bf16[16,2,5120]{2,1,0:T(2,128)(2,1)}), bf16[16,2,5120]{2,1,0:T(2,128)(2,1)S(1)}, u32[]{:S(2)}, u32[]{:S(2)}) async-start(bf16[16,2,5120]{2,1,0:T(2,128)(2,1)} %reshape.102), calls=%async_computation.1 | async-start | bytes 655360 | tf_op jit(solution)/shard_map/all_to_all | solution.py:66
  588.8 3.5 copy-start.2
Sparse Core Ops, SparseCore 0:
  10.1 122.0 all-gather.2
  134.3 127.5 all-gather.4
  264.9 280.1 all-reduce.1
where the time goes:
time: 607 us
  waiting for transfers between devices  495 us (82%)
  starting transfers between devices  26.6 us (4%)
  blocking collectives  20.7 us (3%)
  matrix products  19 us (3%)
  local copies, waits for them, and re-layouts  17.3 us (3%)
  other arithmetic  14.4 us (2%)
  between operations  13.9 us (2%)
    psum x1, waiting for transfers between devices, body(): hidden_total = lax.psum(hidden_grad, 'tensor')  273 us
    all_gather x1, waiting for transfers between devices, body(): lax.all_gather(gate_pre, 'tensor', axis=1, tiled=True)  125 us
    all_gather x1, waiting for transfers between devices, body(): lax.all_gather(up_pre, 'tensor', axis=1, tiled=True)  91.9 us
    all_to_all x1, starting transfers between devices, body(): lax.all_to_all(bin_back, 'expert', split_axis=1, concat_axis=0, tiled=True)  26.5 us
    all_to_all x1, blocking collectives, body(): lax.all_to_all(placed, 'expert', split_axis=0, concat_axis=1, tiled=True)  20.7 us
  transfers between devices with their start and end apart: 4, of which 4 were waited for; matrix products, arithmetic and copies ran while one was open for 5% of the time, Pallas kernels for 0%

commit v1 on v0

v1 whole, which is shorter than its diff:
```python
import functools

import jax
import jax.numpy as jnp
from jax import lax
from jax.experimental import pallas as pl
from jax.experimental.pallas import tpu as pltpu
from jax.sharding import PartitionSpec as P

CAP = 64
F32, BF16 = jnp.float32, jnp.bfloat16
MESH = pl.DeviceIdType.MESH
NT = (((1,), (1,)), ((), ()))

GATE, UP, SUM, ALL = range(4)
X_DOWN, X_GATE, X_UP, X_IN, X_DOWN_GRAD, X_GATE_GRAD, X_UP_GRAD = range(7)


def kernel(
    ne, nz,
    tg, combine, routes, bin_in, gate_pre, up_pre, gate_w, up_w, down_w,
    tok_out, gate_out, up_out, down_out,
    rc_r, rc_c, place, pick, placed, binned, down_x, gate_x, up_x, in_x,
    down_t, in_t, bin_t, part, sum_u, sum_d, first_u, first_d,
    gate_all, up_all, total_all, act_up, act_gate, hidden, gate_delta, up_delta,
    back, back_in, down_s, gate_s, up_s,
    su, ru, sd, rd, out_s, out_r, back_ss, back_r, xs, xr,
):
    e, t = lax.axis_index("expert"), lax.axis_index("tensor")
    xl, z = t // nz, lax.rem(t, nz)
    tokens, width = tg.shape
    top = routes.shape[1]
    fc, bins = gate_pre.shape
    half = fc * nz
    mine = pl.ds(pl.multiple_of(xl * half, 128), half)
    theirs = pl.ds(pl.multiple_of((1 - xl) * half, 128), half)

    def chunk(k):
        return lax.rem(z + k + 2 * nz, nz)

    above = (e, xl * nz + chunk(1))
    below = (e, xl * nz + chunk(-1))
    across = (e, (1 - xl) * nz + z)

    def partner(i):
        rel, de = lax.rem(i, 2), i // 2
        pe = lax.rem(e + de, ne)
        return rel, pe, (pe, lax.rem(xl + rel, 2) * nz + z)

    barrier = pltpu.get_barrier_semaphore()

    def greet(i, _):
        _, _, device = partner(i)
        pl.semaphore_signal(barrier, inc=1, device_id=device, device_id_type=MESH)
        return 0

    lax.fori_loop(1, 2 * ne, greet, 0)
    for device in (above, below):
        pl.semaphore_signal(barrier, inc=1, device_id=device, device_id_type=MESH)
    pl.semaphore_wait(barrier, 2 * ne + 1)

    def hop(ring, s, upward, src, dst):
        return pltpu.make_async_remote_copy(
            src_ref=src, dst_ref=dst,
            send_sem=(su if upward else sd).at[ring, s],
            recv_sem=(ru if upward else rd).at[ring, s],
            device_id=above if upward else below, device_id_type=MESH,
        )

    def gather_send(ring, buf, own, s, upward):
        k = chunk(-s if upward else s)
        hop(ring, s, upward, own if s == 0 else buf.at[k], buf.at[k]).start()

    def gather_recv(ring, buf, s, upward):
        k = chunk(-1 - s if upward else 1 + s)
        hop(ring, s, upward, buf.at[k], buf.at[k]).wait_recv()
        return k

    def exchange(i, src, dst):
        return pltpu.make_async_remote_copy(
            src_ref=src, dst_ref=dst, send_sem=xs.at[i], recv_sem=xr.at[i],
            device_id=across, device_id_type=MESH,
        )

    pre_u, pre_d = nz - 1 - nz // 2, nz // 2
    progress = [0]

    def pump():
        i = progress[0]
        s, ring = i // 2, i % 2
        if s > pre_d:
            return
        progress[0] += 1
        buf, own = ((gate_all, gate_pre), (up_all, up_pre))[ring]
        for upward, n in ((True, pre_u), (False, pre_d)):
            if 0 < s <= n:
                gather_recv(ring, buf, s - 1, upward)
            if s < n:
                gather_send(ring, buf, own, s, upward)
        if ring == 1 and s > 0:
            if s <= pre_u:
                activate(chunk(-s))
            activate(chunk(s))

    def activate(c):
        def rows(r, _):
            at = pl.ds(pl.multiple_of(r * 16, 16), 16)
            g, u = gate_all[c, at, :].astype(F32), up_all[c, at, :].astype(F32)
            s = 1.0 / (1.0 + jnp.exp(-g))
            a = g * s
            act_up[c, at, :] = a
            act_gate[c, at, :] = u * s * (1.0 + g * (1.0 - s))
            hidden[c, at, :] = (a * u).astype(BF16)
            return 0

        lax.fori_loop(0, fc // 16, rows, 0)

    def deltas(c):
        def rows(r, _):
            at = pl.ds(pl.multiple_of(r * 16, 16), 16)
            v = total_all[c, at, :].astype(F32)
            up_delta[c, at, :] = (v * act_up[c, at, :]).astype(BF16)
            gate_delta[c, at, :] = (v * act_gate[c, at, :]).astype(BF16)
            return 0

        lax.fori_loop(0, fc // 16, rows, 0)

    pump()
    pump()
    x_down = exchange(X_DOWN, down_w.at[:, theirs], down_x)
    x_down.start()

    rc_r[...] = jnp.zeros_like(rc_r)
    rc_c[...] = jnp.zeros_like(rc_c)
    rc_r[:, 0:top] = routes[...].astype(F32)
    rc_c[:, 0:top] = combine[...]
    r_t, c_t = rc_r[...].T, rc_c[...].T
    expert_ids = lax.broadcasted_iota(jnp.int32, (ne, tokens), 0).astype(F32)
    named = jnp.zeros((ne, tokens), F32)
    weight = jnp.zeros((ne, tokens), F32)
    for k in range(top):
        hit = r_t[k : k + 1, :] == expert_ids
        named = named + jnp.where(hit, 1.0, 0.0)
        weight = weight + jnp.where(hit, c_t[k : k + 1, :], 0.0)
    before = lax.broadcasted_iota(jnp.int32, (tokens, tokens), 0) < lax.broadcasted_iota(
        jnp.int32, (tokens, tokens), 1
    )
    earlier = jnp.dot(
        named.astype(BF16), jnp.where(before, 1.0, 0.0).astype(BF16), preferred_element_type=F32
    )
    slot = jnp.where(named > 0.5, earlier, -1.0)
    slot_ids = lax.broadcasted_iota(jnp.int32, (CAP, tokens), 0).astype(F32)
    for x in range(ne):
        hit = slot_ids == slot[x : x + 1, :]
        place[x] = jnp.where(hit, 1.0, 0.0)
        w = jnp.where(hit, weight[x : x + 1, :], 0.0)
        hi = w.astype(BF16)
        w = w - hi.astype(F32)
        mid = w.astype(BF16)
        lo = (w - mid.astype(F32)).astype(BF16)
        rows = (
            jnp.dot(hi, tg[...], preferred_element_type=F32)
            + jnp.dot(mid, tg[...], preferred_element_type=F32)
            + jnp.dot(lo, tg[...], preferred_element_type=F32)
        )
        placed[x] = rows.astype(BF16)

    def dispatch(i, _):
        rel, pe, device = partner(i)
        pltpu.make_async_remote_copy(
            src_ref=placed.at[pe], dst_ref=binned.at[rel * ne + e],
            send_sem=out_s, recv_sem=out_r, device_id=device, device_id_type=MESH,
        ).start()
        return 0

    lax.fori_loop(1, 2 * ne, dispatch, 0)
    binned[e] = placed[e]

    pump()
    pump()
    gate_all[z] = gate_pre[...]
    up_all[z] = up_pre[...]
    activate(z)
    down_t[0] = down_w[:, mine].T
    in_t[0] = bin_in[...].T
    pick[...] = place[...].reshape(ne * CAP, tokens).T.astype(BF16)
    pump()
    pump()
    x_down.wait_recv()
    down_t[1] = down_x[...].T

    many = binned.at[pl.ds(0, 2 * ne - 1)]
    pltpu.make_async_copy(many, many, out_r).wait()
    x_gate = exchange(X_GATE, gate_w.at[:, theirs], gate_x)
    x_up = exchange(X_UP, up_w.at[:, theirs], up_x)
    x_in = exchange(X_IN, bin_in, in_x)
    for copy in (x_in, x_gate, x_up):
        copy.start()
    bin_0 = binned[0:ne].reshape(bins, width)
    bin_1 = binned[ne : 2 * ne].reshape(bins, width)
    part[...] = (
        lax.dot_general(down_t[0], bin_0, NT, preferred_element_type=F32)
        + lax.dot_general(down_t[1], bin_1, NT, preferred_element_type=F32)
    ).reshape(nz, fc, bins)

    nu, nd = nz // 2, nz - 1 - nz // 2
    first_u[...] = part[chunk(nu)].astype(BF16)
    hop(SUM, 0, True, first_u, sum_u.at[0]).start()
    first_d[...] = part[chunk(-nd)].astype(BF16)
    hop(SUM, 0, False, first_d, sum_d.at[0]).start()
    bin_t[0] = bin_0.T
    bin_t[1] = bin_1.T
    for s in range(1, nu + 1):
        for upward, n, buf in ((True, nu, sum_u), (False, nd, sum_d)):
            if s <= n:
                hop(SUM, s - 1, upward, buf.at[s - 1], buf.at[s - 1]).wait_recv()
            if s < n:
                c = chunk(nu - s if upward else s - nd)
                buf[s - 1] = (buf[s - 1].astype(F32) + part[c]).astype(BF16)
                hop(SUM, s, upward, buf.at[s - 1], buf.at[s]).start()
        if s < nu:
            pump()
    total_all[z] = (
        part[z] + (sum_u[nu - 1].astype(F32) + sum_d[nd - 1].astype(F32))
    ).astype(BF16)

    for s in range(nu + 1):
        arrived = [z] if s == 0 else []
        for upward, n in ((True, nu), (False, nd)):
            if 0 < s <= n:
                arrived.append(gather_recv(ALL, total_all, s - 1, upward))
            if s < n:
                gather_send(ALL, total_all, total_all.at[z], s, upward)
        while progress[0] < 2 * s + 2 and progress[0] < 2 * pre_d + 2:
            pump()
        pump()
        if s == 2:
            x_in.wait_recv()
            in_t[1] = in_x[...].T
        for c in arrived:
            deltas(c)

    gd = gate_delta[...].reshape(half, bins)
    ud = up_delta[...].reshape(half, bins)
    x_gate.wait_recv()
    x_up.wait_recv()
    for rel in (1, 0):
        gw = gate_x[...] if rel else gate_w[:, mine]
        uw = up_x[...] if rel else up_w[:, mine]
        b_t = jnp.dot(gw, gd, preferred_element_type=F32) + jnp.dot(uw, ud, preferred_element_type=F32)
        back[rel * ne : (rel + 1) * ne] = b_t.T.astype(BF16).reshape(ne, CAP, width)

    def give(i, _):
        rel, pe, device = partner(i)
        pltpu.make_async_remote_copy(
            src_ref=back.at[rel * ne + pe], dst_ref=back_in.at[rel * ne + e],
            send_sem=back_ss, recv_sem=back_r, device_id=device, device_id_type=MESH,
        ).start()
        return 0

    lax.fori_loop(1, 2 * ne, give, 0)
    back_in[e] = back[e]

    copies = []
    for i, left, right, stage, out in (
        (X_GATE_GRAD, in_t, gd, gate_s, gate_out),
        (X_UP_GRAD, in_t, ud, up_s, up_out),
        (X_DOWN_GRAD, bin_t, hidden[...].reshape(half, bins), down_s, down_out),
    ):
        stage[...] = lax.dot_general(left[1], right, NT, preferred_element_type=F32).astype(BF16)
        copy = exchange(i, stage, out.at[:, mine])
        copy.start()
        copies.append(copy)
        out[:, mine] = lax.dot_general(left[0], right, NT, preferred_element_type=F32).astype(BF16)

    many = back_in.at[pl.ds(0, 2 * ne - 1)]
    pltpu.make_async_copy(many, many, back_r).wait()
    token = jnp.dot(
        pick[...], back_in[0:ne].reshape(ne * CAP, width), preferred_element_type=F32
    ) + jnp.dot(pick[...], back_in[ne : 2 * ne].reshape(ne * CAP, width), preferred_element_type=F32)
    tok_out[...] = token.astype(BF16)

    for copy in copies:
        copy.wait_recv()
    many = placed.at[0:1]
    sent = binned.at[pl.ds(0, 2 * ne - 1)]
    pltpu.make_async_copy(sent, sent, out_s).wait()
    sent = back.at[pl.ds(0, 2 * ne - 1)]
    pltpu.make_async_copy(sent, sent, back_ss).wait()
    for copy in [x_down, x_gate, x_up, x_in] + copies:
        copy.wait_send()
    for ring, n_up, n_down in ((GATE, pre_u, pre_d), (UP, pre_u, pre_d), (SUM, nu, nd), (ALL, nu, nd)):
        for s in range(n_up):
            hop(ring, s, True, first_u, first_u).wait_send()
        for s in range(n_down):
            hop(ring, s, False, first_d, first_d).wait_send()


def layer(ne, nz, *args):
    tg, combine, routes, bin_in, gate_pre, up_pre, gate_w, up_w, down_w = args
    bin_in, gate_pre, up_pre, gate_w, up_w, down_w = (
        a.reshape(a.shape[1:]) for a in (bin_in, gate_pre, up_pre, gate_w, up_w, down_w)
    )
    tokens, width = tg.shape
    fc, bins = gate_pre.shape
    half, ff = fc * nz, gate_w.shape[1]
    nu, nd = nz // 2, nz - 1 - nz // 2
    V = pltpu.VMEM
    dma = pltpu.SemaphoreType.DMA
    scratch = [
        V((tokens, 128), F32), V((tokens, 128), F32),
        V((ne, CAP, tokens), F32), V((tokens, ne * CAP), BF16),
        V((ne, CAP, width), BF16), V((2 * ne, CAP, width), BF16),
        V((width, half), BF16), V((width, half), BF16), V((width, half), BF16), V((bins, width), BF16),
        V((2, half, width), BF16), V((2, width, bins), BF16), V((2, width, bins), BF16),
        V((nz, fc, bins), F32),
        V((nu, fc, bins), BF16), V((max(nd, 1), fc, bins), BF16), V((fc, bins), BF16), V((fc, bins), BF16),
        V((nz, fc, bins), BF16), V((nz, fc, bins), BF16), V((nz, fc, bins), BF16),
        V((nz, fc, bins), F32), V((nz, fc, bins), F32), V((nz, fc, bins), BF16),
        V((nz, fc, bins), BF16), V((nz, fc, bins), BF16),
        V((2 * ne, CAP, width), BF16), V((2 * ne, CAP, width), BF16),
        V((width, half), BF16), V((width, half), BF16), V((width, half), BF16),
        dma((4, nu)), dma((4, nu)), dma((4, nu)), dma((4, nu)),
        dma, dma, dma, dma, dma((7,)), dma((7,)),
    ]
    grad = jax.ShapeDtypeStruct((width, ff), BF16)
    vmem = pl.BlockSpec(memory_space=pltpu.VMEM)
    token, gate, up, down = pl.pallas_call(
        functools.partial(kernel, ne, nz),
        out_shape=(jax.ShapeDtypeStruct((tokens, width), BF16), grad, grad, grad),
        in_specs=[vmem] * 9,
        out_specs=(vmem,) * 4,
        scratch_shapes=scratch,
        compiler_params=pltpu.CompilerParams(
            collective_id=0, has_side_effects=True, vmem_limit_bytes=58 * 2**20
        ),
        cost_estimate=pl.CostEstimate(
            flops=12 * width * ff * bins, bytes_accessed=6 * 2**20, transcendentals=half * bins
        ),
    )(tg, combine, routes, bin_in, gate_pre, up_pre, gate_w, up_w, down_w)
    return token, gate[None], up[None], down[None]


def solution(mesh):
    ne, nz = mesh.shape["expert"], mesh.shape["tensor"] // 2
    return jax.shard_map(
        functools.partial(layer, ne, nz),
        mesh=mesh,
        in_specs=(
            P("expert", "tensor"),
            P("expert", None),
            P("expert", None),
            P("expert", None, "tensor"),
            P("expert", "tensor", None),
            P("expert", "tensor", None),
            P("expert", "tensor", None),
            P("expert", "tensor", None),
            P("expert", "tensor", None),
        ),
        out_specs=(
            P("expert", "tensor"),
            P("expert", "tensor", None),
            P("expert", "tensor", None),
            P("expert", "tensor", None),
        ),
        check_vma=False,
    )
```

time: 607 us -> 141 us (0.23)
  the two profiles are of different devices: /device:TPU:1 before, /device:TPU:26 now
where the time goes in v1:
time: 141 us; the launch traced here: 140 us
  Pallas kernels  129 us (91%)
  local copies, waits for them, and re-layouts  10.4 us (7%)
    pallas_call x1, Pallas kernels, layer(): pl.pallas_call(functools.partial(kernel, ne, nz), out_shape=(jax.ShapeDty...  129 us
    unnamed x16, local copies, waits for them, and re-layouts  10.4 us

profile of v1, /device:TPU:26, one launch (start us, length us, event | category | flops | bytes accessed | tf_op | source)
XLA Modules:
  0.0 140.5 jit_solution(13631523176203326964)
XLA Ops:
  0.6 0.0 copy-start.2
  0.6 1.5 %copy.14.tg = bf16[128,160]{1,0:T(8,128)(2,1)} copy(bf16[128,160]{0,1:T(8,128)(2,1)} %param.9) | data formatting | bytes 81920 | tf_op args[0]
  2.2 0.0 copy-done.2
  2.2 0.0 copy-start.3
  2.2 0.7 copy.15.combine
  2.9 0.0 copy-done.3
  2.9 0.7 copy.16.routes
  3.6 2.0 %copy.13 = bf16[1,1024,160]{2,1,0:T(8,128)(2,1)} copy(bf16[1,1024,160]{1,2,0:T(8,128)(2,1)} %param.12) | data formatting | bytes 655360 | tf_op args[3]
  5.6 129.4 %shard_map.120 = (bf16[128,160]{1,0:T(8,128)(2,1)}, bf16[160,1536]{1,0:T(8,128)(2,1)}, bf16[160,1536]{1,0:T(8,128)(2,1)}, bf16[160,1536]{1,0:T(8,128)(2,1)}) custom-call(bf16[128,160]{1,0:T(8,128)(2,1)} %copy.14.tg, f32[128,6]{1,0:T(8,128)} %copy.15.combine, s32[128,6]{1,0:T(8,128)} %copy.16.routes, bf16[1024,160]{1,0:T(8,128)(2,1)} %bitcast.9, ...), custom_call_target="tpu_custom_call" | custom-call | flops 3019898880 | bytes 6291456 | tf_op jit(solution)/shard_map/pallas_call | solution.py:328
  135.0 1.6 %copy.17 = bf16[128,160]{0,1:T(8,128)(2,1)} copy(bf16[128,160]{1,0:T(8,128)(2,1)} %get-tuple-element.12) | data formatting | bytes 81920
  136.6 0.0 copy-start.1
  136.6 1.9 %copy.21 = bf16[1,160,1536]{2,1,0:T(8,128)(2,1)} copy(bf16[1,160,1536]{2,1,0:T(8,128)(2,1)} %bitcast.12) | data formatting | bytes 983040
  138.5 0.0 copy-done.1
  138.5 0.0 copy-start
  138.5 0.8 copy.22
  139.3 0.4 copy-done
  139.7 0.8 copy.23
Async XLA Ops:
  0.6 1.5 %copy-start.2 = (f32[128,6]{0,1:T(8,128)S(1)}, f32[128,6]{0,1:T(8,128)}, u32[]{:S(2)}) copy-start(f32[128,6]{0,1:T(8,128)} %param.10) | copy-start | bytes 9220
  2.2 0.7 copy-start.3
  136.6 1.9 %copy-start.1 = (bf16[160,1536]{1,0:T(8,128)(2,1)S(1)}, bf16[160,1536]{1,0:T(8,128)(2,1)}, u32[]{:S(2)}) copy-start(bf16[160,1536]{1,0:T(8,128)(2,1)} %get-tuple-element.10) | copy-start | bytes 1474564
  138.5 1.2 copy-start

commit v2 on v0

v2 whole, which is shorter than its diff:
```python
import functools

import jax
import jax.numpy as jnp
from jax import lax
from jax.experimental import pallas as pl
from jax.experimental.pallas import tpu as pltpu
from jax.sharding import PartitionSpec as P

CAP = 64
LANES = 128
F32, BF16 = jnp.float32, jnp.bfloat16
MESH = pl.DeviceIdType.MESH
NT = (((1,), (1,)), ((), ()))

GATE, UP, SUM, ALL = 0, 1, (2, 3), (4, 5)
EARLY, BESIDE = 6, 1
LAG = 0


def nt(left, right):
    return lax.dot_general(left, right, NT, preferred_element_type=F32)


def nn(left, right):
    return jnp.dot(left, right, preferred_element_type=F32)


def kernel(
    ne, nz,
    tg, combine, routes, bin_in_h, gate_pre, up_pre, gate_w, up_w, down_w,
    tok_out, gate_out, up_out, down_out,
    bin_in, gate_m, up_m, down_m,
    place, pick, split, tail_t, placed, binned, bin_r, back, back_in, tok_r,
    down_x, gate_x, up_x, in_x, down_t, down_tr, bin_t, part,
    sum_u, sum_d, first_u, first_d, gate_all, up_all, total_all,
    act_up, act_gate, hidden, gate_delta, up_delta,
    down_s, strip, strip_in, grad_t, grad_tr,
    su, ru, sd, rd, out_s, out_r, back_s, back_r, xs, xr, ss, sr, ls,
):
    e, t = lax.axis_index("expert"), lax.axis_index("tensor")
    xl, z = t // nz, lax.rem(t, nz)
    width, tokens = tg.shape
    top = routes.shape[0]
    fc, bins = gate_pre.shape
    half = fc * nz
    rest = width - LANES
    groups = LANES // rest
    rows_g = CAP // groups
    mine = pl.ds(pl.multiple_of(xl * half, LANES), half)
    theirs = pl.ds(pl.multiple_of((1 - xl) * half, LANES), half)

    def chunk(k):
        return lax.rem(z + k + 2 * nz, nz)

    above = (e, xl * nz + chunk(1))
    below = (e, xl * nz + chunk(-1))
    across = (e, (1 - xl) * nz + z)

    def partner(i):
        rel, de = lax.rem(i, 2), i // 2
        pe = lax.rem(e + de, ne)
        return rel, pe, (pe, lax.rem(xl + rel, 2) * nz + z)

    local = [
        pltpu.make_async_copy(src, dst, ls.at[i])
        for i, (src, dst) in enumerate((
            (gate_pre, gate_all.at[z]), (up_pre, up_all.at[z]), (down_w.at[:, mine], down_m),
            (bin_in_h, bin_in), (gate_w.at[:, mine], gate_m), (up_w.at[:, mine], up_m),
        ))
    ]
    for copy in local:
        copy.start()

    barrier = pltpu.get_barrier_semaphore()

    def greet(i, _):
        _, _, device = partner(i)
        pl.semaphore_signal(barrier, inc=1, device_id=device, device_id_type=MESH)
        return 0

    for device in (above, below):
        pl.semaphore_signal(barrier, inc=1, device_id=device, device_id_type=MESH)
    lax.fori_loop(1, 2 * ne, greet, 0)

    expert_ids = lax.broadcasted_iota(jnp.int32, (ne, tokens), 0)
    named = jnp.zeros((ne, tokens), F32)
    weight = jnp.zeros((ne, tokens), F32)
    for k in range(top):
        hit = routes[k : k + 1, :] == expert_ids
        named = named + jnp.where(hit, 1.0, 0.0)
        weight = weight + jnp.where(hit, combine[k : k + 1, :], 0.0)
    before = lax.broadcasted_iota(jnp.int32, (tokens, tokens), 0) < lax.broadcasted_iota(
        jnp.int32, (tokens, tokens), 1
    )
    earlier = nn(named.astype(BF16), jnp.where(before, 1.0, 0.0).astype(BF16))
    slot = jnp.where(named > 0.5, earlier, -1.0)
    slot_ids = lax.broadcasted_iota(jnp.int32, (CAP, tokens), 0).astype(F32)
    for x in range(ne):
        hit = slot_ids == slot[x : x + 1, :]
        place[x] = jnp.where(hit, 1.0, 0.0)
        w = jnp.where(hit, weight[x : x + 1, :], 0.0)
        hi = w.astype(BF16)
        w = w - hi.astype(F32)
        mid = w.astype(BF16)
        split[0, x] = hi
        split[1, x] = mid
        split[2, x] = (w - mid.astype(F32)).astype(BF16)
    tail_t[...] = jnp.zeros_like(tail_t)
    for j in range(groups):
        tail_t[j * rest : (j + 1) * rest, j * tokens : (j + 1) * tokens] = tg[LANES:width, :]
    head, tail = 0.0, 0.0
    for k in range(3):
        head += nt(split[k].reshape(ne * CAP, tokens), tg[0:LANES, :])
        packed = jnp.concatenate(
            [split[k, :, j * rows_g : (j + 1) * rows_g, :].reshape(ne * rows_g, tokens) for j in range(groups)],
            axis=1,
        )
        tail += nt(packed, tail_t[...])
    placed[:, 0:CAP, :] = head.astype(BF16).reshape(ne, CAP, LANES)
    placed[:, CAP:, :] = tail.astype(BF16).reshape(ne, rows_g, LANES)

    pl.semaphore_wait(barrier, 2 * ne + 1)

    sends, due = [], {}

    def start(key, copy):
        copy.start()
        sends.append(copy)
        due[key] = copy

    def hop(ring, s, upward, src, dst):
        start((ring, s, upward), pltpu.make_async_remote_copy(
            src_ref=src, dst_ref=dst,
            send_sem=(su if upward else sd).at[ring, s],
            recv_sem=(ru if upward else rd).at[ring, s],
            device_id=above if upward else below, device_id_type=MESH,
        ))

    def exchange(key, src, dst, send_sem, recv_sem):
        start(key, pltpu.make_async_remote_copy(
            src_ref=src, dst_ref=dst, send_sem=send_sem, recv_sem=recv_sem,
            device_id=across, device_id_type=MESH,
        ))

    def landed(key):
        due.pop(key).wait_recv()

    bulk = {}

    def to_all(key, src, dst, send_sem, recv_sem, only=None):
        def one(i, _):
            rel, pe, device = partner(i if only is None else 2 * i + only)
            pltpu.make_async_remote_copy(
                src_ref=src(rel, pe), dst_ref=dst.at[rel * ne + e],
                send_sem=send_sem, recv_sem=recv_sem, device_id=device, device_id_type=MESH,
            ).start()
            return 0

        first, last = (1, 2 * ne) if only is None else (1 - only, ne)
        lax.fori_loop(first, last, one, 0)
        many = dst.at[pl.ds((only or 0) * ne, last - first)]
        bulk[key] = pltpu.make_async_copy(many, many, recv_sem)
        bulk[key, "sent"] = pltpu.make_async_copy(many, many, send_sem)

    def gather_send(ring, buf, own, s, upward):
        k = chunk(-s if upward else s)
        hop(ring, s, upward, own if s == 0 else buf.at[k], buf.at[k])

    pre_u, pre_d = nz - 1 - nz // 2, nz // 2
    nu, nd = nz // 2, nz - 1 - nz // 2
    progress = [0]

    def pump():
        i = progress[0]
        s, ring = i // 2, i % 2
        if s > pre_d:
            return
        progress[0] += 1
        buf, own = ((gate_all, gate_pre), (up_all, up_pre))[ring]
        for upward, n in ((False, pre_d), (True, pre_u)):
            if 0 < s <= n:
                landed((ring, s - 1, upward))
            if s < n:
                gather_send(ring, buf, own, s, upward)
        if ring == 1 and s > 0:
            if s <= pre_u:
                activate(chunk(-s))
            activate(chunk(s))

    def activate(c):
        def rows(r, _):
            at = pl.ds(pl.multiple_of(r * 16, 16), 16)
            g, u = gate_all[c, at, :].astype(F32), up_all[c, at, :].astype(F32)
            s = 1.0 / (1.0 + jnp.exp(-g))
            a = g * s
            act_up[c, at, :] = a
            act_gate[c, at, :] = u * s * (1.0 + g * (1.0 - s))
            hidden[c, at, :] = (a * u).astype(BF16)
            return 0

        lax.fori_loop(0, fc // 16, rows, 0)

    def deltas(c, h):
        at = halves[h]
        v = total_all[c, :, at].astype(F32)
        up_delta[c, :, at] = (v * act_up[c, :, at]).astype(BF16)
        gate_delta[c, :, at] = (v * act_gate[c, :, at]).astype(BF16)

    halves = [pl.ds(h * (bins // 2), bins // 2) for h in (0, 1)]

    def step(h, i):
        at = halves[h]
        for upward, n, buf, first in ((True, nu, sum_u, first_u), (False, nd, sum_d, first_d)):
            if 0 < i <= n:
                landed((SUM[h], i - 1, upward))
            if i < n:
                c = chunk(nu - i if upward else i - nd)
                if i == 0:
                    first[:, at] = part[c, :, at].astype(BF16)
                else:
                    buf[i - 1, :, at] = (buf[i - 1, :, at].astype(F32) + part[c, :, at]).astype(BF16)
                source = buf.at[i - 1, :, at] if i else first.at[:, at]
                hop(SUM[h], i, upward, source, buf.at[i, :, at])
        if i < nu:
            return
        s = i - nu
        if s == 0:
            total_all[z, :, at] = (
                part[z, :, at] + (sum_u[nu - 1, :, at].astype(F32) + sum_d[nd - 1, :, at].astype(F32))
            ).astype(BF16)
        for upward, n in ((True, nu), (False, nd)):
            if 0 < s <= n:
                landed((ALL[h], s - 1, upward))
            if s < n:
                total = total_all.at[chunk(-s if upward else s), :, at]
                hop(ALL[h], s, upward, total, total)


    def work():
        to_all("out", lambda rel, pe: placed.at[pe], binned, out_s, out_r)
        pump()
        pump()
        exchange("down", down_w.at[:, theirs], down_x, xs.at[0], xr.at[0])
        binned[e] = placed[e]

        pump()
        for i in (0, 1):
            local[i].wait()
        activate(z)
        pump()
        pick[...] = place[...].reshape(ne * CAP, tokens).T.astype(BF16)
        pump()
        local[2].wait()
        down_t[:, 0:LANES] = down_m[0:LANES, :].T
        pump()
        landed("down")
        down_t[:, LANES:] = down_x[0:LANES, :].T
        down_tr[...] = jnp.concatenate([down_m[LANES:, :], down_x[LANES:, :]], axis=0).T
        while progress[0] < EARLY:
            pump()
        bulk.pop("out").wait()

        exchange("in", bin_in_h, in_x, xs.at[1], xr.at[1])
        exchange("gate", gate_w.at[:, theirs], gate_x, xs.at[2], xr.at[2])
        exchange("up", up_w.at[:, theirs], up_x, xs.at[3], xr.at[3])
        for rel in (0, 1):
            for j in range(groups):
                bin_r[:, j * rows_g : (j + 1) * rows_g, rel * rest : (rel + 1) * rest] = binned[
                    rel * ne : (rel + 1) * ne, CAP:, j * rest : (j + 1) * rest
                ]
        heads = [binned[rel * ne : (rel + 1) * ne, 0:CAP, :].reshape(bins, LANES) for rel in (0, 1)]
        part[...] = (
            nt(down_t[...], jnp.concatenate(heads, axis=1))
            + nt(down_tr[...], bin_r[...].reshape(bins, 2 * rest))
        ).reshape(nz, fc, bins)

        step(0, 0)
        for rel in (0, 1):
            bin_t[rel, 0:LANES] = binned[rel * ne : (rel + 1) * ne, 0:CAP, :].reshape(bins, LANES).T
        tails = bin_r[...].reshape(bins, 2 * rest).T
        for rel in (0, 1):
            bin_t[rel, LANES:] = tails[rel * rest : (rel + 1) * rest]
        strips = []
        for slot_no in range(2 * nu + 1 + LAG):
            if 0 < slot_no <= 2 * nu:
                step(0, slot_no)
            if slot_no >= LAG:
                step(1, slot_no - LAG)
            if slot_no % BESIDE == BESIDE - 1:
                pump()
            for h in (0, 1):
                s = slot_no - LAG * h - nu
                if s < 0 or s > nu:
                    continue
                arrived = [0] if s == 0 else [k for k in (-s, s) if -nu <= k <= nd]
                while progress[0] < min(2 * s + 2, 2 * pre_d + 2):
                    pump()
                for k in arrived:
                    deltas(chunk(k), h)
                if h == 0:
                    continue
                if s == 0:
                    local[3].wait()
                    landed("in")
                strips.append(arrived)
                pieces = []
                for k in arrived:
                    pieces += [gate_delta[chunk(k)], up_delta[chunk(k)]]
                n = len(pieces)
                made = nt(jnp.concatenate(pieces, axis=0), in_x[...]).astype(BF16)
                strip[s, 0 : n * fc, :] = made[:, 0:LANES]
                for j in range(n):
                    strip[s, n * fc : (n + 1) * fc, j * rest : (j + 1) * rest] = made[j * fc : (j + 1) * fc, LANES:]
                sent = pl.ds(0, (n + 1) * fc)
                exchange(("strip", s), strip.at[s, sent], strip_in.at[s, sent], ss.at[s], sr.at[s])
                if progress[0] == 2 * pre_d + 2 and "down_grad" not in due:
                    down_s[...] = nt(bin_t[1], hidden[...].reshape(half, bins)).astype(BF16)
                    exchange("down_grad", down_s, down_out.at[:, mine], xs.at[4], xr.at[4])

        gd = gate_delta[...].reshape(half, bins)
        ud = up_delta[...].reshape(half, bins)
        local[4].wait()
        local[5].wait()
        landed("gate")
        landed("up")
        for rel in (1, 0):
            b_t = nn((gate_x if rel else gate_m)[...], gd) + nn((up_x if rel else up_m)[...], ud)
            at = slice(rel * ne, (rel + 1) * ne)
            b_t = b_t.astype(BF16)
            back[at, 0:CAP, :] = b_t[0:LANES].T.reshape(ne, CAP, LANES)
            tail = b_t[LANES:].T.reshape(ne, groups, rows_g, rest)
            for j in range(groups):
                back[at, CAP:, j * rest : (j + 1) * rest] = tail[:, j]
            to_all(("back", rel), lambda rel, pe: back.at[rel * ne + pe], back_in, back_s.at[rel], back_r.at[rel], rel)
        back_in[e] = back[e]

        gate_out[:, mine] = nt(bin_in[...], gd).astype(BF16)
        up_out[:, mine] = nt(bin_in[...], ud).astype(BF16)
        down_out[:, mine] = nt(bin_t[0], hidden[...].reshape(half, bins)).astype(BF16)
        for s, arrived in enumerate(strips):
            landed(("strip", s))
            n = 2 * len(arrived)
            for i, k in enumerate(arrived):
                c = chunk(k)
                for a in (0, 1):
                    j = 2 * i + a
                    grad_t[a, c] = strip_in[s, j * fc : (j + 1) * fc, :]
                    grad_tr[c, :, a * rest : (a + 1) * rest] = strip_in[
                        s, n * fc : (n + 1) * fc, j * rest : (j + 1) * rest
                    ]
        tails = grad_tr[...].reshape(half, 2 * rest).T
        for a, out in enumerate((gate_out, up_out)):
            out[0:LANES, theirs] = grad_t[a].reshape(half, LANES).T
            out[LANES:, theirs] = tails[a * rest : (a + 1) * rest]

        for rel in (1, 0):
            bulk.pop(("back", rel)).wait()
        for rel in (0, 1):
            for j in range(groups):
                tok_r[:, j * rows_g : (j + 1) * rows_g, rel * rest : (rel + 1) * rest] = back_in[
                    rel * ne : (rel + 1) * ne, CAP:, j * rest : (j + 1) * rest
                ]
        token = 0.0
        for rel in (0, 1):
            token += nn(pick[...], back_in[rel * ne : (rel + 1) * ne, 0:CAP, :].reshape(ne * CAP, LANES))
        tok_out[0:LANES, :] = token.T.astype(BF16)
        tail = nn(pick[...], tok_r[...].reshape(ne * CAP, 2 * rest)).T
        tok_out[LANES:, :] = (tail[0:rest] + tail[rest:]).astype(BF16)
        landed("down_grad")

    work()

    for copy in bulk.values():
        copy.wait()
    for copy in sends:
        copy.wait_send()


def finish(*refs):
    n = len(refs) // 3
    ins, outs, held, sems = refs[0:n], refs[n : 2 * n], refs[2 * n : 3 * n], refs[-1]
    reads = [pltpu.make_async_copy(ins[i], held[i], sems.at[i]) for i in range(n)]
    writes = [pltpu.make_async_copy(held[i], outs[i], sems.at[n + i]) for i in range(n)]
    for copy in reads:
        copy.start()
    for i in range(n):
        reads[i].wait()
        writes[i].start()
    for copy in writes:
        copy.wait()


def layer(ne, nz, *args):
    tg, combine, routes, bin_in, gate_pre, up_pre, gate_w, up_w, down_w = args
    bin_in, gate_pre, up_pre, gate_w, up_w, down_w = (
        a.reshape(a.shape[1:]) for a in (bin_in, gate_pre, up_pre, gate_w, up_w, down_w)
    )
    tg, combine, routes, bin_in = tg.T, combine.T, routes.T, bin_in.T
    width, tokens = tg.shape
    fc, bins = gate_pre.shape
    half, ff = fc * nz, gate_w.shape[1]
    nu, nd = nz // 2, nz - 1 - nz // 2
    rest = width - LANES
    groups = LANES // rest
    block = CAP + CAP // groups
    dma = pltpu.SemaphoreType.DMA

    def v(*shape, dtype=BF16):
        return pltpu.VMEM(shape, dtype)

    scratch = [
        v(width, bins), v(width, half), v(width, half), v(width, half),
        v(ne, CAP, tokens, dtype=F32), v(tokens, ne * CAP), v(3, ne, CAP, tokens), v(LANES, groups * tokens),
        v(ne, block, LANES), v(2 * ne, block, LANES), v(ne, CAP, 2 * rest),
        v(2 * ne, block, LANES), v(2 * ne, block, LANES), v(ne, CAP, 2 * rest),
        v(width, half), v(width, half), v(width, half), v(width, bins),
        v(half, 2 * LANES), v(half, 2 * rest), v(2, width, bins), v(nz, fc, bins, dtype=F32),
        v(nu, fc, bins), v(nd, fc, bins), v(fc, bins), v(fc, bins),
        v(nz, fc, bins), v(nz, fc, bins), v(nz, fc, bins),
        v(nz, fc, bins, dtype=F32), v(nz, fc, bins, dtype=F32), v(nz, fc, bins),
        v(nz, fc, bins), v(nz, fc, bins),
        v(width, half), v(nu + 1, 5 * fc, LANES), v(nu + 1, 5 * fc, LANES),
        v(2, nz, fc, LANES), v(nz, fc, 2 * rest),
        dma((6, nu)), dma((6, nu)), dma((6, nu)), dma((6, nu)),
        dma, dma, dma((2,)), dma((2,)), dma((5,)), dma((5,)), dma((nu + 1,)), dma((nu + 1,)), dma((6,)),
    ]
    grad = jax.ShapeDtypeStruct((width, ff), BF16)
    outs = (jax.ShapeDtypeStruct((width, tokens), BF16), grad, grad, grad)
    vmem, hbm = pl.BlockSpec(memory_space=pltpu.VMEM), pl.BlockSpec(memory_space=pl.ANY)
    made = pl.pallas_call(
        functools.partial(kernel, ne, nz),
        out_shape=outs,
        in_specs=[vmem] * 3 + [hbm] * 6,
        out_specs=(vmem,) * 4,
        scratch_shapes=scratch,
        compiler_params=pltpu.CompilerParams(
            collective_id=0, has_side_effects=True, vmem_limit_bytes=58 * 2**20
        ),
        cost_estimate=pl.CostEstimate(
            flops=12 * width * ff * bins, bytes_accessed=6 * 2**20, transcendentals=half * bins
        ),
    )(tg, combine, routes, bin_in, gate_pre, up_pre, gate_w, up_w, down_w)
    made = pl.pallas_call(
        finish,
        out_shape=outs,
        in_specs=[hbm] * 4,
        out_specs=(hbm,) * 4,
        scratch_shapes=[v(width, tokens), v(width, ff), v(width, ff), v(width, ff), dma((8,))],
    )(*made)
    token, gate, up, down = made
    return token.T, gate[None], up[None], down[None]


def solution(mesh):
    ne, nz = mesh.shape["expert"], mesh.shape["tensor"] // 2
    return jax.shard_map(
        functools.partial(layer, ne, nz),
        mesh=mesh,
        in_specs=(
            P("expert", "tensor"),
            P("expert", None),
            P("expert", None),
            P("expert", None, "tensor"),
            P("expert", "tensor", None),
            P("expert", "tensor", None),
            P("expert", "tensor", None),
            P("expert", "tensor", None),
            P("expert", "tensor", None),
        ),
        out_specs=(
            P("expert", "tensor"),
            P("expert", "tensor", None),
            P("expert", "tensor", None),
            P("expert", "tensor", None),
        ),
        check_vma=False,
    )
```

time: 607 us -> 111 us (0.18)
  waiting for transfers between devices: 495 us -> 0 us
  Pallas kernels: 0 us -> 111 us
  starting transfers between devices: 26.6 us -> 0 us
  blocking collectives: 20.7 us -> 0 us
  matrix products: 19 us -> 0 us
  local copies, waits for them, and re-layouts: 17.3 us -> 0 us
  other arithmetic: 14.4 us -> 0 us
  between operations: 13.9 us -> 0.64 us
    psum x1 -> x0, waiting for transfers between devices: 273 us -> none  [body(): hidden_total = lax.psum(hidden_grad, 'tensor')]
    all_gather x2 -> x0, waiting for transfers between devices: 217 us -> none  [the longest x1 125 us: body(): lax.all_gather(gate_pre, 'tensor', axis=1, tiled=True)]
    pallas_call x0 -> x2, Pallas kernels: none -> 111 us  [the longest x1 108 us: layer(): pl.pallas_call(functools.partial(kernel, ne, nz), out_shape=outs, in_spec...]
    all_to_all x1 -> x0, starting transfers between devices: 26.5 us -> none  [body(): lax.all_to_all(bin_back, 'expert', split_axis=1, concat_axis=0, tiled=True)]
    all_to_all x1 -> x0, blocking collectives: 20.7 us -> none  [body(): lax.all_to_all(placed, 'expert', split_axis=0, concat_axis=1, tiled=True)]
    dot_general x8 -> x0, matrix products: 19 us -> none  [the longest x1 5.93 us: body(): jnp.einsum('ebd,efb->edf', binned, hidden, preferred_element_type=jnp.flo...]
    all_gather x2 -> x0, local copies, waits for them, and re-layouts: 9.4 us -> none  [the longest x1 4.72 us: body(): lax.all_gather(up_pre, 'tensor', axis=1, tiled=True)]
    convert_element_type x2 -> x0, other arithmetic: 6.18 us -> none  [the longest x1 6.18 us: activate(): gate_delta = (hidden_grad * up_vals * sigmoid_gate * (1.0 + gate_vals * (...]
  transfers between devices with their start and end apart: 4 -> 0, of which waited for: 4 -> 0; matrix products, arithmetic and copies ran while one was open for 5% -> 0% of each run, Pallas kernels for 0% -> 0%
where the time goes in v2:
time: 111 us
  Pallas kernels  111 us (100%)
    pallas_call x1, Pallas kernels, layer(): pl.pallas_call(functools.partial(kernel, ne, nz), out_shape=outs, in_spec...  108 us
    pallas_call x1, Pallas kernels, layer(): pl.pallas_call(finish, out_shape=outs, in_specs=[hbm] * 4, out_specs=(hbm...  2.23 us

profile of v2, /device:TPU:1, one launch (start us, length us, event | category | flops | bytes accessed | tf_op | source)
XLA Modules:
  0.0 111.2 jit_solution(5236069837182704762)
XLA Ops:
  0.6 108.3 %shard_map.120 = (bf16[160,128]{1,0:T(8,128)(2,1)}, bf16[160,1536]{1,0:T(8,128)(2,1)}, bf16[160,1536]{1,0:T(8,128)(2,1)}, bf16[160,1536]{1,0:T(8,128)(2,1)}) custom-call(bf16[160,128]{1,0:T(8,128)(2,1)} %bitcast.24, f32[6,128]{1,0:T(8,128)} %bitcast.26, s32[6,128]{1,0:T(8,128)} %bitcast.27, bf16[160,1024]{1,0:T(8,128)(2,1)} %bitcast.21, ...), custom_call_target="tpu_custom_call" | custom-call | flops 3019898880 | bytes 6291456 | tf_op jit(solution)/shard_map/pallas_call | solution.py:431
  108.9 2.2 %shard_map.121 = (bf16[160,128]{1,0:T(8,128)(2,1)}, bf16[160,1536]{1,0:T(8,128)(2,1)}, bf16[160,1536]{1,0:T(8,128)(2,1)}, bf16[160,1536]{1,0:T(8,128)(2,1)}) custom-call(bf16[160,128]{1,0:T(8,128)(2,1)} %get-tuple-element.12.refs_0_, bf16[160,1536]{1,0:T(8,128)(2,1)} %get-tuple-element.13.refs_1_, bf16[160,1536]{1,0:T(8,128)(2,1)} %get-tuple-element.14.refs_2_, ...), custom_call_target="tpu_custom_call" | custom-call | tf_op jit(solution)/shard_map/pallas_call | solution.py:444

commit v3 on v2

--- a/solution.py
+++ b/solution.py
@@ -14,7 +14,7 @@
 NT = (((1,), (1,)), ((), ()))
 
 GATE, UP, SUM, ALL = 0, 1, (2, 3), (4, 5)
-EARLY, BESIDE = 6, 1
+EARLY, SLOTS = 6, (0, 1) * 4 + (1,) * 9
 LAG = 0
 
 
@@ -28,11 +28,11 @@
 
 def kernel(
     ne, nz,
-    tg, combine, routes, bin_in_h, gate_pre, up_pre, gate_w, up_w, down_w,
+    tg_h, combine_h, routes_h, bin_in_h, gate_pre, up_pre, gate_w, up_w, down_w,
     tok_out, gate_out, up_out, down_out,
-    bin_in, gate_m, up_m, down_m,
+    tg, combine, routes, bin_in, gate_m, up_m, down_m,
     place, pick, split, tail_t, placed, binned, bin_r, back, back_in, tok_r,
-    down_x, gate_x, up_x, in_x, down_t, down_tr, bin_t, part,
+    down_x, gate_x, up_x, in_x, down_t, down_tr, bin_w, bin_t, part,
     sum_u, sum_d, first_u, first_d, gate_all, up_all, total_all,
     act_up, act_gate, hidden, gate_delta, up_delta,
     down_s, strip, strip_in, grad_t, grad_tr,
@@ -40,8 +40,8 @@
 ):
     e, t = lax.axis_index("expert"), lax.axis_index("tensor")
     xl, z = t // nz, lax.rem(t, nz)
-    width, tokens = tg.shape
-    top = routes.shape[0]
+    width, tokens = tg_h.shape
+    top = routes_h.shape[0]
     fc, bins = gate_pre.shape
     half = fc * nz
     rest = width - LANES
@@ -67,9 +67,10 @@
         for i, (src, dst) in enumerate((
             (gate_pre, gate_all.at[z]), (up_pre, up_all.at[z]), (down_w.at[:, mine], down_m),
             (bin_in_h, bin_in), (gate_w.at[:, mine], gate_m), (up_w.at[:, mine], up_m),
+            (routes_h, routes), (combine_h, combine), (tg_h, tg),
         ))
     ]
-    for copy in local:
+    for copy in local[6:] + local[:6]:
         copy.start()
 
     barrier = pltpu.get_barrier_semaphore()
@@ -83,6 +84,8 @@
         pl.semaphore_signal(barrier, inc=1, device_id=device, device_id_type=MESH)
     lax.fori_loop(1, 2 * ne, greet, 0)
 
+    for copy in local[6:]:
+        copy.wait()
     expert_ids = lax.broadcasted_iota(jnp.int32, (ne, tokens), 0)
     named = jnp.zeros((ne, tokens), F32)
     weight = jnp.zeros((ne, tokens), F32)
@@ -269,11 +272,18 @@
                 bin_r[:, j * rows_g : (j + 1) * rows_g, rel * rest : (rel + 1) * rest] = binned[
                     rel * ne : (rel + 1) * ne, CAP:, j * rest : (j + 1) * rest
                 ]
-        heads = [binned[rel * ne : (rel + 1) * ne, 0:CAP, :].reshape(bins, LANES) for rel in (0, 1)]
-        part[...] = (
-            nt(down_t[...], jnp.concatenate(heads, axis=1))
-            + nt(down_tr[...], bin_r[...].reshape(bins, 2 * rest))
-        ).reshape(nz, fc, bins)
+        for rel in (0, 1):
+            bin_w[:, rel * LANES : (rel + 1) * LANES] = binned[rel * ne : (rel + 1) * ne, 0:CAP, :].reshape(bins, LANES)
+
+        def products(ks):
+            at = [pl.ds(pl.multiple_of(chunk(k) * fc, 16), fc) for k in ks]
+            made = nt(jnp.concatenate([down_t[a, :] for a in at], axis=0), bin_w[...]) + nt(
+                jnp.concatenate([down_tr[a, :] for a in at], axis=0), bin_r[...].reshape(bins, 2 * rest)
+            )
+            for i, k in enumerate(ks):
+                part[chunk(k)] = made[i * fc : (i + 1) * fc]
+
+        products([nu, -nd])
 
         step(0, 0)
         for rel in (0, 1):
@@ -283,11 +293,13 @@
             bin_t[rel, LANES:] = tails[rel * rest : (rel + 1) * rest]
         strips = []
         for slot_no in range(2 * nu + 1 + LAG):
+            if 0 < slot_no <= nu:
+                products([k for k in (nu - slot_no, slot_no - nd) if k > 0 or slot_no < nd] if slot_no < nu else [0])
             if 0 < slot_no <= 2 * nu:
                 step(0, slot_no)
             if slot_no >= LAG:
                 step(1, slot_no - LAG)
-            if slot_no % BESIDE == BESIDE - 1:
+            for _ in range(SLOTS[slot_no]):
                 pump()
             for h in (0, 1):
                 s = slot_no - LAG * h - nu
@@ -410,12 +422,13 @@
         return pltpu.VMEM(shape, dtype)
 
     scratch = [
+        v(*tg.shape), v(*combine.shape, dtype=F32), v(*routes.shape, dtype=jnp.int32),
         v(width, bins), v(width, half), v(width, half), v(width, half),
         v(ne, CAP, tokens, dtype=F32), v(tokens, ne * CAP), v(3, ne, CAP, tokens), v(LANES, groups * tokens),
         v(ne, block, LANES), v(2 * ne, block, LANES), v(ne, CAP, 2 * rest),
         v(2 * ne, block, LANES), v(2 * ne, block, LANES), v(ne, CAP, 2 * rest),
         v(width, half), v(width, half), v(width, half), v(width, bins),
-        v(half, 2 * LANES), v(half, 2 * rest), v(2, width, bins), v(nz, fc, bins, dtype=F32),
+        v(half, 2 * LANES), v(half, 2 * rest), v(bins, 2 * LANES), v(2, width, bins), v(nz, fc, bins, dtype=F32),
         v(nu, fc, bins), v(nd, fc, bins), v(fc, bins), v(fc, bins),
         v(nz, fc, bins), v(nz, fc, bins), v(nz, fc, bins),
         v(nz, fc, bins, dtype=F32), v(nz, fc, bins, dtype=F32), v(nz, fc, bins),
@@ -423,7 +436,7 @@
         v(width, half), v(nu + 1, 5 * fc, LANES), v(nu + 1, 5 * fc, LANES),
         v(2, nz, fc, LANES), v(nz, fc, 2 * rest),
         dma((6, nu)), dma((6, nu)), dma((6, nu)), dma((6, nu)),
-        dma, dma, dma((2,)), dma((2,)), dma((5,)), dma((5,)), dma((nu + 1,)), dma((nu + 1,)), dma((6,)),
+        dma, dma, dma((2,)), dma((2,)), dma((5,)), dma((5,)), dma((nu + 1,)), dma((nu + 1,)), dma((9,)),
     ]
     grad = jax.ShapeDtypeStruct((width, ff), BF16)
     outs = (jax.ShapeDtypeStruct((width, tokens), BF16), grad, grad, grad)
@@ -431,7 +444,7 @@
     made = pl.pallas_call(
         functools.partial(kernel, ne, nz),
         out_shape=outs,
-        in_specs=[vmem] * 3 + [hbm] * 6,
+        in_specs=[pl.BlockSpec(memory_space=pltpu.HBM)] * 9,
         out_specs=(vmem,) * 4,
         scratch_shapes=scratch,
         compiler_params=pltpu.CompilerParams(

time: 111 us -> 108 us (0.973)
  Pallas kernels: 111 us -> 107 us
    pallas_call x1, Pallas kernels: 108 us -> 105 us  [layer(): pl.pallas_call(functools.partial(kernel, ne, nz), out_shape=outs, in_spec...]
where the time goes in v3:
time: 108 us; the launch traced here: 107 us
  Pallas kernels  107 us (99%)
    pallas_call x1, Pallas kernels, layer(): pl.pallas_call(functools.partial(kernel, ne, nz), out_shape=outs, in_spec...  105 us
    pallas_call x1, Pallas kernels, layer(): pl.pallas_call(finish, out_shape=outs, in_specs=[hbm] * 4, out_specs=(hbm...  2.23 us

profile of v3, /device:TPU:1, one launch (start us, length us, event | category | flops | bytes accessed | tf_op | source)
XLA Modules:
  0.0 107.4 jit_solution(3974128386881091431)
XLA Ops:
  0.6 104.6 %shard_map.120 = (bf16[160,128]{1,0:T(8,128)(2,1)}, bf16[160,1536]{1,0:T(8,128)(2,1)}, bf16[160,1536]{1,0:T(8,128)(2,1)}, bf16[160,1536]{1,0:T(8,128)(2,1)}) custom-call(bf16[160,128]{1,0:T(8,128)(2,1)} %bitcast.24, f32[6,128]{1,0:T(8,128)} %bitcast.26, s32[6,128]{1,0:T(8,128)} %bitcast.27, bf16[160,1024]{1,0:T(8,128)(2,1)} %bitcast.21, ...), custom_call_target="tpu_custom_call" | custom-call | flops 3019898880 | bytes 6291456 | tf_op jit(solution)/shard_map/pallas_call | solution.py:444
  105.2 2.2 %shard_map.121 = (bf16[160,128]{1,0:T(8,128)(2,1)}, bf16[160,1536]{1,0:T(8,128)(2,1)}, bf16[160,1536]{1,0:T(8,128)(2,1)}, bf16[160,1536]{1,0:T(8,128)(2,1)}) custom-call(bf16[160,128]{1,0:T(8,128)(2,1)} %get-tuple-element.12.refs_0_, bf16[160,1536]{1,0:T(8,128)(2,1)} %get-tuple-element.13.refs_1_, bf16[160,1536]{1,0:T(8,128)(2,1)} %get-tuple-element.14.refs_2_, ...), custom_call_target="tpu_custom_call" | custom-call | tf_op jit(solution)/shard_map/pallas_call | solution.py:457

commit v4 on v3

--- a/solution.py
+++ b/solution.py
@@ -153,7 +153,13 @@
 
     def to_all(key, src, dst, send_sem, recv_sem, only=None):
         def one(i, _):
-            rel, pe, device = partner(i if only is None else 2 * i + only)
+            if only is None:
+                i = lax.rem(i + ne - 1, 2 * ne - 1) + 1
+            elif only == 0:
+                i = 2 * (lax.rem(i + ne // 2 - 2, ne - 1) + 1)
+            else:
+                i = 2 * lax.rem(i + ne // 2, ne) + 1
+            rel, pe, device = partner(i)
             pltpu.make_async_remote_copy(
                 src_ref=src(rel, pe), dst_ref=dst.at[rel * ne + e],
                 send_sem=send_sem, recv_sem=recv_sem, device_id=device, device_id_type=MESH,
@@ -241,9 +247,9 @@
 
 
     def work():
+        pump()
+        pump()
         to_all("out", lambda rel, pe: placed.at[pe], binned, out_s, out_r)
-        pump()
-        pump()
         exchange("down", down_w.at[:, theirs], down_x, xs.at[0], xr.at[0])
         binned[e] = placed[e]
 

time: 108 us -> 108 us (level)
  no operation moved by 1% of the time
where the time goes in v4:
time: 108 us
  Pallas kernels  107 us (99%)
    pallas_call x1, Pallas kernels, layer(): pl.pallas_call(functools.partial(kernel, ne, nz), out_shape=outs, in_spec...  105 us
    pallas_call x1, Pallas kernels, layer(): pl.pallas_call(finish, out_shape=outs, in_specs=[hbm] * 4, out_specs=(hbm...  2.23 us

profile of v4, /device:TPU:1, one launch (start us, length us, event | category | flops | bytes accessed | tf_op | source)
XLA Modules:
  0.0 107.9 jit_solution(13509647115515189938)
XLA Ops:
  0.6 105.0 %shard_map.120 = (bf16[160,128]{1,0:T(8,128)(2,1)}, bf16[160,1536]{1,0:T(8,128)(2,1)}, bf16[160,1536]{1,0:T(8,128)(2,1)}, bf16[160,1536]{1,0:T(8,128)(2,1)}) custom-call(bf16[160,128]{1,0:T(8,128)(2,1)} %bitcast.24, f32[6,128]{1,0:T(8,128)} %bitcast.26, s32[6,128]{1,0:T(8,128)} %bitcast.27, bf16[160,1024]{1,0:T(8,128)(2,1)} %bitcast.21, ...), custom_call_target="tpu_custom_call" | custom-call | flops 3019898880 | bytes 6291456 | tf_op jit(solution)/shard_map/pallas_call | solution.py:450
  105.7 2.2 %shard_map.121 = (bf16[160,128]{1,0:T(8,128)(2,1)}, bf16[160,1536]{1,0:T(8,128)(2,1)}, bf16[160,1536]{1,0:T(8,128)(2,1)}, bf16[160,1536]{1,0:T(8,128)(2,1)}) custom-call(bf16[160,128]{1,0:T(8,128)(2,1)} %get-tuple-element.12.refs_0_, bf16[160,1536]{1,0:T(8,128)(2,1)} %get-tuple-element.13.refs_1_, bf16[160,1536]{1,0:T(8,128)(2,1)} %get-tuple-element.14.refs_2_, ...), custom_call_target="tpu_custom_call" | custom-call | tf_op jit(solution)/shard_map/pallas_call | solution.py:463
